TPU v7x, 256 devices: a whole 4x4x8 slice. The times are simulated.
256 devices in a mesh: rows: 64 (over x, y, z_lo, core), vec: 4 (over z_hi).
Axes of the slice: x: 4, y: 4, z: 8 (z_hi: 4, z_lo: 2; z = z_hi * 2 + z_lo), core: 2. Of those that a mesh axis runs over, the one named last changes fastest.
Arguments:
- walkers: bfloat16 [1024, 4800], P('rows'), may hold values from -6 to 6
- inv_intersection: bfloat16 [32, 150, 150], replicated, may hold values from -0.5 to 0.5
- rotated: bfloat16 [1024, 1024, 150], P('vec', 'rows'), may hold values from -0.875 to 0.875
- cholesky: bfloat16 [1024, 1024, 1024], P('vec', 'rows'), may hold values from -0.03125 to 0.03125
- field_noise: float32 [32, 1024], P(None, 'vec'), may hold values from -6 to 6
Outputs:
- fields: float32 [32, 1024], P(None, 'vec')
- propagated: bfloat16 [1024, 4800], P('rows', 'vec')
All inputs are finite; a program needn't handle non-finite values.
Results may differ from a plain program's by a relative error of at most 0.014.
Values may be sent and summed in bfloat16 or wider, within the bound.
A program may use at most 128 MiB of HBM per device.

v0:
```python
import functools

import jax
import jax.numpy as jnp
from jax import lax
from jax.experimental import pallas as pl
from jax.experimental.pallas import tpu as pltpu
from jax.sharding import PartitionSpec as P

MESH = pl.DeviceIdType.MESH
ORDER = 4
LANES = 128
TILE = 256
PARTS = 5

time_root = 0.1


def ceil_to(value, unit):
    return -(-value // unit) * unit


def place(nb, r):
    if nb == 2:
        return r % 2, r // 2
    x, y, low = r // 16, (r // 4) % 4, r % 4
    return ((y + y // 2) % 2) * 4 + low, x * 2 + y // 2


def device(nb, a, b):
    if nb == 2:
        return b * 2 + a
    x, half = b // 2, b % 2
    return x * 16 + (2 * half + (a // 4 + half) % 2) * 4 + a % 4


def kernel(
    dims,
    walkers_hbm,
    inverse_hbm,
    rotated_hbm,
    chol_hbm,
    noise_hbm,
    fields_ref,
    out_ref,
    walkers,
    inverse,
    rotated,
    chol,
    noise,
    wide_low,
    wide_high,
    mixed,
    mixed_diag,
    part,
    phi,
    spread,
    order,
    wide,
    diag,
    fb_one,
    fb_two,
    fb_all,
    phi_block,
    terms,
    send_far,
    send_right,
    send_left,
    hold_right,
    hold_left,
    own,
    far_left,
    far_right,
    op_own,
    op_early,
    op_late,
    turned_operator,
    result,
    landed,
    load_sem,
    fb_send,
    fb_recv,
    phi_sem,
    term_send,
    term_recv,
    far_send,
    far_recv,
    early_send,
    early_recv,
    own_send,
    own_recv,
    late_send,
    late_recv,
    out_sem,
):
    na, nb, nh, rows, electrons = dims
    half = nb // 2
    block = nb * rows
    depth = chol.shape[0]
    orbitals = chol.shape[1]
    padded = terms.shape[1]
    r = lax.axis_index("rows")
    h = lax.axis_index("vec")
    a, b = place(nb, r)

    def a_at(i):
        return sum(((a // bit) % 2 if not (na - i) // bit % 2 else 1 - (a // bit) % 2) * bit for bit in (4, 2, 1) if bit < na)

    def b_at(i):
        if nb == 2:
            return 1 - b
        step, turn = ((2, 1), (1, 1), (3, 1), (2, 0), (1, 0), (3, 0), (0, 1))[i - 1]
        return (b // 2 + step) % 4 * 2 + (1 - b % 2 if turn else b % 2)

    def a_peer(i):
        return (device(nb, a_at(i), b), h)

    def b_peer(i):
        return (device(nb, a, b_at(i)), h)

    def h_peer(i):
        return (r, (h + i) % nh)

    def send(src, dst, send_sem, recv_sem, peer):
        copy = pltpu.make_async_remote_copy(
            src_ref=src, dst_ref=dst, send_sem=send_sem, recv_sem=recv_sem, device_id=peer, device_id_type=MESH
        )
        copy.start()

    def wait(span, sem):
        pltpu.make_async_copy(span, span, sem).wait()

    def chunk(c):
        return (pl.ds(pl.multiple_of((c // 2) * 8, 8), 8), pl.ds(pl.multiple_of((c % 2) * LANES, LANES), LANES))

    pairs = ((walkers_hbm, walkers), (inverse_hbm, inverse), (rotated_hbm, rotated), (chol_hbm, chol), (noise_hbm, noise))
    loads = [pltpu.make_async_copy(src, dst, load_sem.at[i]) for i, (src, dst) in enumerate(pairs)]
    for load in loads:
        load.start()

    barrier = pltpu.get_barrier_semaphore()
    def owner(j, step):
        return (device(nb, a, j), (h + step) % nh)

    peers = [a_peer(i) for i in range(1, na)] + [b_peer(i) for i in range(1, nb)]
    peers += [owner(j, step) for j in range(nb) for step in (1, nh - 1)]
    for peer in peers:
        pl.semaphore_signal(barrier, inc=1, device_id=peer, device_id_type=MESH)
    def fill(k, _):
        row = lax.broadcasted_iota(jnp.int32, (spread.shape[0], TILE), 0)
        lane = lax.broadcasted_iota(jnp.int32, (spread.shape[0], TILE), 1)
        here = row == (TILE // rows) * k + lane // rows
        spread[:, pl.ds(pl.multiple_of(k * TILE, TILE), TILE)] = jnp.where(here, 1.0, 0.0).astype(jnp.bfloat16)
        return 0

    lax.fori_loop(0, depth // TILE, fill, 0)

    count = mixed.shape[0]
    span = electrons * rows
    loads[1].wait()
    wide_low[: electrons * count, :] = inverse[:, :, :LANES].astype(jnp.float32).reshape(electrons * count, LANES)
    wide_high[: electrons * count, : electrons - LANES] = (
        inverse[:, :, LANES:].astype(jnp.float32).reshape(electrons * count, electrons - LANES)
    )
    loads[0].wait()
    for w in range(count):
        low = wide_low[pl.ds(w, ceil_to(electrons, 8), stride=count), :]
        high = wide_high[pl.ds(w, ceil_to(electrons, 8), stride=count), :]
        matrix = jnp.concatenate([low, high], axis=1).astype(jnp.bfloat16)[:electrons, :electrons]
        mixed[w] = jnp.dot(
            walkers[:, w * electrons : (w + 1) * electrons], matrix, preferred_element_type=jnp.float32
        ).astype(jnp.bfloat16)
    for start in range(0, span, TILE):
        here = pl.ds(start, min(TILE, span - start))
        spaced = jnp.dot(
            mixed[...].reshape(count * rows, electrons), spread[:electrons, here], preferred_element_type=jnp.float32
        )
        p = lax.broadcasted_iota(jnp.int32, spaced.shape, 0) % rows
        lane = lax.broadcasted_iota(jnp.int32, spaced.shape, 1) % rows
        mixed_diag[:, here] = jnp.where(p == lane, spaced, 0.0).astype(jnp.bfloat16)
    phi[:, :, LANES:] = jnp.zeros((nb, rows, phi.shape[2] - LANES), jnp.bfloat16)
    for k in range(nh):

        @pl.when(h == k)
        def _():
            for j in range(nb):
                start = (k * nb + j) * electrons
                phi[j, :, :electrons] = walkers[:, start : start + electrons]

    pl.semaphore_wait(barrier, len(peers))

    for i in range(1, nb):
        send(phi.at[b_at(i)], phi_block.at[b], phi_sem.at[0], phi_sem.at[1], b_peer(i))
    phi_block[b] = phi[b]
    loads[2].wait()
    by_row = jnp.dot(mixed_diag[...], rotated[...], preferred_element_type=jnp.float32)
    part[...] = jnp.sum(by_row.reshape(count, rows, by_row.shape[1]), axis=1)

    for i in range(1, na):
        send(part.at[chunk(a_at(i))], fb_one.at[i], fb_send.at[0], fb_recv.at[0], a_peer(i))

    def arrange(k, _):
        lane = lax.broadcasted_iota(jnp.int32, (1, block), 1)
        source = device(nb, k, lane // rows) * rows + lane % rows
        row = lax.broadcasted_iota(jnp.int32, (orbitals, block), 0)
        here = pl.ds(pl.multiple_of(k * block, block), block)
        order[:, here] = jnp.where(row == source, 1.0, 0.0).astype(jnp.bfloat16)
        return 0

    lax.fori_loop(0, na, arrange, 0)

    fb_chunks = fb_one.at[pl.ds(1, na - 1)]
    wait(fb_chunks, fb_recv.at[0])
    total = part[chunk(a)]
    for i in range(1, na):
        total = total + fb_one[i]
    fb_two[b] = total
    for i in range(1, nb):
        send(fb_two.at[b], fb_two.at[b], fb_send.at[1], fb_recv.at[1], b_peer(i))

    wait(phi_block.at[pl.ds(0, nb - 1)], phi_sem.at[1])
    mine = pl.ds(pl.multiple_of(a * block, block), block)
    turned = jnp.transpose(phi_block[...].reshape(block, phi_block.shape[2]).astype(jnp.float32))
    first = turned[:padded, :]
    terms[0, :, mine] = first.astype(jnp.bfloat16)

    def some(c):
        return pl.ds(c * (padded // PARTS), padded // PARTS)

    def share(k, c):
        there = terms.at[k, some(c), mine]
        for i in range(1, na):
            send(there, there, term_send.at[k], term_recv.at[k, c], a_peer(i))

    for c in range(PARTS):
        share(0, c)

    wait(fb_two.at[pl.ds(0, nb - 1)], fb_recv.at[1])
    total = fb_two[0]
    for i in range(1, nb):
        total = total + fb_two[i]
    fb_all[chunk(a)] = total
    for i in range(1, na):
        send(fb_all.at[chunk(a)], fb_all.at[chunk(a)], fb_send.at[2], fb_recv.at[2], a_peer(i))

    wait(fb_chunks, fb_recv.at[2])
    loads[4].wait()
    fields = noise[...] - time_root * fb_all[...]
    fields_ref[...] = fields
    scaled = (-time_root * fields).astype(jnp.bfloat16)

    wide[...] = jnp.dot(scaled, spread[...], preferred_element_type=jnp.float32)
    loads[3].wait()

    lower, upper = pl.ds(0, half), pl.ds(half, half)
    width = min(TILE, orbitals)
    tiles = orbitals // width

    def build(slot, c):
        p = lax.broadcasted_iota(jnp.int32, (rows, depth), 0)
        lane = lax.broadcasted_iota(jnp.int32, (rows, depth), 1)
        for w in range(nb):
            row = jnp.broadcast_to(wide[pl.ds(c * nb + w, 1), :], (rows, depth))
            diag[slot, w * rows : (w + 1) * rows, :] = jnp.where(p == lane % rows, row, 0.0).astype(jnp.bfloat16)

    def multiply(slot, store, some_spots):
        for here in some_spots:
            product = jnp.dot(diag[slot], chol[:, here], preferred_element_type=jnp.float32)
            store(here, product.reshape(nb, rows, width))

    def store_far(here, value):
        send_far[:, :, here] = value.astype(jnp.bfloat16)

    def store_right(here, value):
        hold_right[:, :, here] = value[:half]
        send_right[half:, :, here] = value[half:].astype(jnp.bfloat16)

    def store_left(here, value):
        send_left[:half, :, here] = value[:half].astype(jnp.bfloat16)
        hold_left[:, :, here] = value[half:]

    def store_own(here, value):
        own[:, :, here] = value.astype(jnp.bfloat16)

    spots = [pl.ds(n * width, width) for n in range(tiles)]
    right, left = h_peer(1), h_peer(nh - 1)
    build(0, (h + 2) % nh)
    for n, here in enumerate(spots):
        if n < 2:
            multiply(0, store_far, spots[:1] if n == 0 else spots[1:])
        send(send_far.at[lower, :, here], far_left.at[:, :, here], far_send.at[0], far_recv.at[0, n], right)
        send(send_far.at[upper, :, here], far_right.at[:, :, here], far_send.at[1], far_recv.at[1, n], left)
    build(1, (h + 1) % nh)
    build(0, (h + nh - 1) % nh)
    multiply(1, store_right, spots)
    build(1, h)
    multiply(0, store_left, spots)
    multiply(1, store_own, spots)
    for j in range(half):
        k = half + j
        send(send_right.at[k], op_early.at[b], early_send, early_recv, owner(k, 1))
        send(send_left.at[j], op_early.at[b], early_send, early_recv, owner(j, nh - 1))
    for i in range(1, nb):
        send(own.at[b_at(i)], op_own.at[b], own_send, own_recv, b_peer(i))
    op_own[b] = own[b]

    for n, here in enumerate(spots):
        wait(far_left.at[:, :, here], far_recv.at[0, n])
        send_right[:half, :, here] = (hold_right[:, :, here] + far_left[:, :, here].astype(jnp.float32)).astype(
            jnp.bfloat16
        )
        for j in range(half):
            send(send_right.at[j, :, here], op_late.at[b, :, here], late_send, late_recv.at[n], owner(j, 1))
        wait(far_right.at[:, :, here], far_recv.at[1, n])
        send_left[half:, :, here] = (hold_left[:, :, here] + far_right[:, :, here].astype(jnp.float32)).astype(
            jnp.bfloat16
        )
        for k in range(half, nb):
            send(send_left.at[k, :, here], op_late.at[b, :, here], late_send, late_recv.at[n], owner(k, nh - 1))

    wait(op_own.at[pl.ds(0, nb - 1)], own_recv)
    wait(op_early, early_recv)
    turned = jnp.zeros((block, orbitals), jnp.float32)
    for n, here in enumerate(spots):
        wait(op_late.at[:, :, here], late_recv.at[n])
        value = op_own[:, :, here].astype(jnp.float32) + op_early[:, :, here].astype(jnp.float32)
        value = (value + op_late[:, :, here].astype(jnp.float32)).astype(jnp.bfloat16)
        turned = turned + jnp.dot(value.reshape(block, width), order[here, :], preferred_element_type=jnp.float32)
    turned_operator[...] = turned.astype(jnp.bfloat16)

    summed = [first[c * (padded // PARTS) : (c + 1) * (padded // PARTS)] for c in range(PARTS)]
    for degree in range(1, ORDER + 1):
        for c in range(PARTS):
            wait(terms.at[degree - 1, some(c), pl.ds(0, (na - 1) * block)], term_recv.at[degree - 1, c])
            product = lax.dot_general(
                terms[degree - 1, some(c), :],
                turned_operator[...],
                (((1,), (1,)), ((), ())),
                preferred_element_type=jnp.float32,
            )
            term = (product / degree).astype(jnp.bfloat16)
            if degree < ORDER:
                terms[degree, some(c), mine] = term
                share(degree, c)
            summed[c] = summed[c] + term.astype(jnp.float32)

    tall = jnp.concatenate([*summed, jnp.zeros((result.shape[2] - padded, block), jnp.float32)], axis=0)
    result[...] = jnp.transpose(tall).astype(jnp.bfloat16).reshape(result.shape)
    for i in range(1, nb):
        send(result.at[b_at(i)], landed.at[b], out_sem.at[0], out_sem.at[1], b_peer(i))
    landed[b] = result[b]
    wait(landed.at[pl.ds(0, nb - 1)], out_sem.at[1])
    for j in range(nb):
        out_ref[:, j * electrons : (j + 1) * electrons] = landed[j, :, :electrons]

    for i in range(3):
        wait(fb_chunks, fb_send.at[i])
    wait(phi.at[pl.ds(0, nb - 1)], phi_sem.at[0])
    for k in range(ORDER):
        wait(terms.at[k, :, pl.ds(0, (na - 1) * block)], term_send.at[k])
    wait(far_left, far_send.at[0])
    wait(far_right, far_send.at[1])
    wait(op_early, early_send)
    wait(op_late, late_send)
    wait(op_own.at[pl.ds(0, nb - 1)], own_send)
    wait(result.at[pl.ds(0, nb - 1)], out_sem.at[0])


def local(na, nb, nh, walkers, inv_intersection, rotated, cholesky, field_noise):
    walker_count, electrons = inv_intersection.shape[:2]
    rows = walkers.shape[0]
    vectors, _, orbitals = cholesky.shape
    wide_electrons = ceil_to(electrons, LANES)
    padded = ceil_to(electrons, 16)
    half = nb // 2
    bf16, f32 = jnp.bfloat16, jnp.float32
    depth = vectors * rows
    dma = pltpu.SemaphoreType.DMA
    vmem = pl.BlockSpec(memory_space=pltpu.VMEM)
    piece = (nb, rows, orbitals)
    fields, propagated = pl.pallas_call(
        functools.partial(kernel, (na, nb, nh, rows, electrons)),
        out_shape=(
            jax.ShapeDtypeStruct((walker_count, vectors), f32),
            jax.ShapeDtypeStruct((rows, nb * electrons), bf16),
        ),
        in_specs=[pl.BlockSpec(memory_space=pltpu.HBM)] * 5,
        out_specs=(vmem, vmem),
        scratch_shapes=[
            pltpu.VMEM(walkers.shape, bf16),
            pltpu.VMEM((electrons, walker_count, electrons), bf16),
            pltpu.VMEM((electrons * rows, vectors), bf16),
            pltpu.VMEM((depth, orbitals), bf16),
            pltpu.VMEM((walker_count, vectors), f32),
            pltpu.VMEM((ceil_to(electrons, 8) * walker_count, LANES), f32),
            pltpu.VMEM((ceil_to(electrons, 8) * walker_count, LANES), f32),
            pltpu.VMEM((walker_count, rows, electrons), bf16),
            pltpu.VMEM((walker_count * rows, electrons * rows), bf16),
            pltpu.VMEM((walker_count, vectors), f32),
            pltpu.VMEM((nb, rows, wide_electrons), bf16),
            pltpu.VMEM((vectors, depth), bf16),
            pltpu.VMEM((orbitals, orbitals), bf16),
            pltpu.VMEM((walker_count, depth), f32),
            pltpu.VMEM((2, nb * rows, depth), bf16),
            pltpu.VMEM((na, 8, LANES), f32),
            pltpu.VMEM((nb, 8, LANES), f32),
            pltpu.VMEM((walker_count, vectors), f32),
            pltpu.VMEM((nb, rows, wide_electrons), bf16),
            pltpu.VMEM((ORDER, padded, orbitals), bf16),
            pltpu.VMEM(piece, bf16),
            pltpu.VMEM(piece, bf16),
            pltpu.VMEM(piece, bf16),
            pltpu.VMEM((half, rows, orbitals), f32),
            pltpu.VMEM((half, rows, orbitals), f32),
            pltpu.VMEM(piece, bf16),
            pltpu.VMEM((half, rows, orbitals), bf16),
            pltpu.VMEM((half, rows, orbitals), bf16),
            pltpu.VMEM(piece, bf16),
            pltpu.VMEM(piece, bf16),
            pltpu.VMEM(piece, bf16),
            pltpu.VMEM((nb * rows, orbitals), bf16),
            pltpu.VMEM((nb, rows, wide_electrons), bf16),
            pltpu.VMEM((nb, rows, wide_electrons), bf16),
            dma((5,)),
            dma((3,)),
            dma((3,)),
            dma((2,)),
            dma((ORDER,)),
            dma((ORDER, PARTS)),
            dma((2,)),
            dma((2, 4)),
            dma,
            dma,
            dma,
            dma,
            dma,
            dma((4,)),
            dma((2,)),
        ],
        compiler_params=pltpu.CompilerParams(
            collective_id=0, has_side_effects=True, vmem_limit_bytes=48 * 1024 * 1024
        ),
    )(
        *(
            pltpu.with_memory_space_constraint(array, pltpu.HBM)
            for array in (
                walkers,
                jnp.transpose(inv_intersection, (1, 0, 2)),
                jnp.transpose(rotated, (2, 1, 0)).reshape(electrons * rows, vectors),
                cholesky.reshape(depth, orbitals),
                field_noise,
            )
        )
    )
    return fields, propagated


def solution(mesh):
    nh = mesh.shape["vec"]
    nb = 8 if mesh.shape["rows"] == 64 else 2
    na = mesh.shape["rows"] // nb
    placed = (P("rows", None), P(), P("vec", "rows", None), P("vec", "rows", None), P(None, "vec"))
    return jax.shard_map(
        functools.partial(local, na, nb, nh),
        mesh=mesh,
        in_specs=placed,
        out_specs=(P(None, "vec"), P("rows", "vec")),
        check_vma=False,
    )
```

profile of v0, /device:TPU:1, one launch (start us, length us, event | category | flops | bytes accessed | tf_op | source)
XLA Modules:
  0.0 68.0 jit_solution(15862194259684860972)
XLA Ops:
  0.6 66.1 %shard_map.68 = (f32[32,256]{1,0:T(8,128)S(1)}, bf16[16,1200]{1,0:T(8,128)(2,1)S(1)}) custom-call(bf16[16,4800]{1,0:T(8,128)(2,1)} %walkers_hbm.1, bf16[150,32,150]{2,1,0:T(8,128)(2,1)} %bitcast.6, bf16[2400,256]{1,0:T(8,128)(2,1)} %bitcast.7, bf16[4096,1024]{1,0:T(8,128)(2,1)} %bitcast.5, f32[32,256]{1,0:T(8,128)} %noise_hbm.1), custom_call_target="tpu_custom_call" | custom-call | tf_op jit(solution)/shard_map/pallas_call | solution.py:381
  66.7 0.6 copy.9
  67.3 0.6 copy.10
where the time goes:
time: 68 us
  Pallas kernels  66.1 us (97%)
  local copies, waits for them, and re-layouts  1.23 us (2%)
    pallas_call x1, Pallas kernels, local(): pl.pallas_call(functools.partial(kernel, (na, nb, nh, rows, electrons)),...  66.1 us

commit v1 on v0

--- a/solution.py
+++ b/solution.py
@@ -48,8 +48,7 @@
     rotated,
     chol,
     noise,
-    wide_low,
-    wide_high,
+    by_walker,
     mixed,
     mixed_diag,
     part,
@@ -135,8 +134,8 @@
 
     pairs = ((walkers_hbm, walkers), (inverse_hbm, inverse), (rotated_hbm, rotated), (chol_hbm, chol), (noise_hbm, noise))
     loads = [pltpu.make_async_copy(src, dst, load_sem.at[i]) for i, (src, dst) in enumerate(pairs)]
-    for load in loads:
-        load.start()
+    for i in (1, 0, 2):
+        loads[i].start()
 
     barrier = pltpu.get_barrier_semaphore()
     def owner(j, step):
@@ -157,18 +156,26 @@
 
     count = mixed.shape[0]
     span = electrons * rows
+    to = lax.broadcasted_iota(jnp.int32, (8 * count, 8 * count), 0)
+    source = lax.broadcasted_iota(jnp.int32, (8 * count, 8 * count), 1)
+    gather = jnp.where(source == (to % 8) * count + to // 8, 1.0, 0.0).astype(jnp.bfloat16)
     loads[1].wait()
-    wide_low[: electrons * count, :] = inverse[:, :, :LANES].astype(jnp.float32).reshape(electrons * count, LANES)
-    wide_high[: electrons * count, : electrons - LANES] = (
-        inverse[:, :, LANES:].astype(jnp.float32).reshape(electrons * count, electrons - LANES)
-    )
+
+    def eight(f):
+        size = min(8, electrons - f)
+        if size <= 0:
+            return jnp.zeros((count, 8, electrons), jnp.float32)
+        taken = inverse[f : f + size].reshape(size * count, electrons)
+        return jnp.dot(gather[:, : size * count], taken, preferred_element_type=jnp.float32).reshape(count, 8, electrons)
+
+    for f in range(0, electrons, 16):
+        by_walker[:, f : f + 16, :] = jnp.concatenate([eight(f), eight(f + 8)], axis=1).astype(jnp.bfloat16)
     loads[0].wait()
     for w in range(count):
-        low = wide_low[pl.ds(w, ceil_to(electrons, 8), stride=count), :]
-        high = wide_high[pl.ds(w, ceil_to(electrons, 8), stride=count), :]
-        matrix = jnp.concatenate([low, high], axis=1).astype(jnp.bfloat16)[:electrons, :electrons]
         mixed[w] = jnp.dot(
-            walkers[:, w * electrons : (w + 1) * electrons], matrix, preferred_element_type=jnp.float32
+            walkers[:, w * electrons : (w + 1) * electrons],
+            by_walker[w, :electrons, :],
+            preferred_element_type=jnp.float32,
         ).astype(jnp.bfloat16)
     for start in range(0, span, TILE):
         here = pl.ds(start, min(TILE, span - start))
@@ -178,6 +185,17 @@
         p = lax.broadcasted_iota(jnp.int32, spaced.shape, 0) % rows
         lane = lax.broadcasted_iota(jnp.int32, spaced.shape, 1) % rows
         mixed_diag[:, here] = jnp.where(p == lane, spaced, 0.0).astype(jnp.bfloat16)
+    loads[3].start()
+    loads[4].start()
+    loads[2].wait()
+    by_row = jnp.dot(mixed_diag[...], rotated[...], preferred_element_type=jnp.float32)
+    part[...] = jnp.sum(by_row.reshape(count, rows, by_row.shape[1]), axis=1)
+
+    pl.semaphore_wait(barrier, len(peers))
+
+    for i in range(1, na):
+        send(part.at[chunk(a_at(i))], fb_one.at[i], fb_send.at[0], fb_recv.at[0], a_peer(i))
+
     phi[:, :, LANES:] = jnp.zeros((nb, rows, phi.shape[2] - LANES), jnp.bfloat16)
     for k in range(nh):
 
@@ -187,17 +205,9 @@
                 start = (k * nb + j) * electrons
                 phi[j, :, :electrons] = walkers[:, start : start + electrons]
 
-    pl.semaphore_wait(barrier, len(peers))
-
     for i in range(1, nb):
         send(phi.at[b_at(i)], phi_block.at[b], phi_sem.at[0], phi_sem.at[1], b_peer(i))
     phi_block[b] = phi[b]
-    loads[2].wait()
-    by_row = jnp.dot(mixed_diag[...], rotated[...], preferred_element_type=jnp.float32)
-    part[...] = jnp.sum(by_row.reshape(count, rows, by_row.shape[1]), axis=1)
-
-    for i in range(1, na):
-        send(part.at[chunk(a_at(i))], fb_one.at[i], fb_send.at[0], fb_recv.at[0], a_peer(i))
 
     def arrange(k, _):
         lane = lax.broadcasted_iota(jnp.int32, (1, block), 1)
@@ -392,8 +402,7 @@
             pltpu.VMEM((electrons * rows, vectors), bf16),
             pltpu.VMEM((depth, orbitals), bf16),
             pltpu.VMEM((walker_count, vectors), f32),
-            pltpu.VMEM((ceil_to(electrons, 8) * walker_count, LANES), f32),
-            pltpu.VMEM((ceil_to(electrons, 8) * walker_count, LANES), f32),
+            pltpu.VMEM((walker_count, ceil_to(electrons, 16), electrons), bf16),
             pltpu.VMEM((walker_count, rows, electrons), bf16),
             pltpu.VMEM((walker_count * rows, electrons * rows), bf16),
             pltpu.VMEM((walker_count, vectors), f32),

time: 68 us -> 65.8 us (0.968)
  Pallas kernels: 66.1 us -> 63.8 us
    pallas_call x1, Pallas kernels: 66.1 us -> 63.8 us  [local(): pl.pallas_call(functools.partial(kernel, (na, nb, nh, rows, electrons)),...]
where the time goes in v1:
time: 65.8 us; the launch traced here: 65.7 us
  Pallas kernels  63.8 us (97%)
  local copies, waits for them, and re-layouts  1.23 us (2%)
    pallas_call x1, Pallas kernels, local(): pl.pallas_call(functools.partial(kernel, (na, nb, nh, rows, electrons)),...  63.8 us

profile of v1, /device:TPU:1, one launch (start us, length us, event | category | flops | bytes accessed | tf_op | source)
XLA Modules:
  0.0 65.7 jit_solution(3057975482838560950)
XLA Ops:
  0.6 63.8 %shard_map.68 = (f32[32,256]{1,0:T(8,128)S(1)}, bf16[16,1200]{1,0:T(8,128)(2,1)S(1)}) custom-call(bf16[16,4800]{1,0:T(8,128)(2,1)} %walkers_hbm.1, bf16[150,32,150]{2,1,0:T(8,128)(2,1)} %bitcast.6, bf16[2400,256]{1,0:T(8,128)(2,1)} %bitcast.7, bf16[4096,1024]{1,0:T(8,128)(2,1)} %bitcast.5, f32[32,256]{1,0:T(8,128)} %noise_hbm.1), custom_call_target="tpu_custom_call" | custom-call | tf_op jit(solution)/shard_map/pallas_call | solution.py:391
  64.5 0.6 copy.9
  65.1 0.6 copy.10

commit v2 on v1

--- a/solution.py
+++ b/solution.py
@@ -59,7 +59,6 @@
     diag,
     fb_one,
     fb_two,
-    fb_all,
     phi_block,
     terms,
     send_far,
@@ -129,9 +128,6 @@
     def wait(span, sem):
         pltpu.make_async_copy(span, span, sem).wait()
 
-    def chunk(c):
-        return (pl.ds(pl.multiple_of((c // 2) * 8, 8), 8), pl.ds(pl.multiple_of((c % 2) * LANES, LANES), LANES))
-
     pairs = ((walkers_hbm, walkers), (inverse_hbm, inverse), (rotated_hbm, rotated), (chol_hbm, chol), (noise_hbm, noise))
     loads = [pltpu.make_async_copy(src, dst, load_sem.at[i]) for i, (src, dst) in enumerate(pairs)]
     for i in (1, 0, 2):
@@ -193,8 +189,9 @@
 
     pl.semaphore_wait(barrier, len(peers))
 
+    fb_one[a] = part[...].astype(jnp.bfloat16)
     for i in range(1, na):
-        send(part.at[chunk(a_at(i))], fb_one.at[i], fb_send.at[0], fb_recv.at[0], a_peer(i))
+        send(fb_one.at[a], fb_one.at[a], fb_send.at[0], fb_recv.at[0], a_peer(i))
 
     phi[:, :, LANES:] = jnp.zeros((nb, rows, phi.shape[2] - LANES), jnp.bfloat16)
     for k in range(nh):
@@ -219,12 +216,11 @@
 
     lax.fori_loop(0, na, arrange, 0)
 
-    fb_chunks = fb_one.at[pl.ds(1, na - 1)]
-    wait(fb_chunks, fb_recv.at[0])
-    total = part[chunk(a)]
+    wait(fb_one.at[pl.ds(0, na - 1)], fb_recv.at[0])
+    total = fb_one[0].astype(jnp.float32)
     for i in range(1, na):
-        total = total + fb_one[i]
-    fb_two[b] = total
+        total = total + fb_one[i].astype(jnp.float32)
+    fb_two[b] = total.astype(jnp.bfloat16)
     for i in range(1, nb):
         send(fb_two.at[b], fb_two.at[b], fb_send.at[1], fb_recv.at[1], b_peer(i))
 
@@ -246,16 +242,11 @@
         share(0, c)
 
     wait(fb_two.at[pl.ds(0, nb - 1)], fb_recv.at[1])
-    total = fb_two[0]
+    force_bias = fb_two[0].astype(jnp.float32)
     for i in range(1, nb):
-        total = total + fb_two[i]
-    fb_all[chunk(a)] = total
-    for i in range(1, na):
-        send(fb_all.at[chunk(a)], fb_all.at[chunk(a)], fb_send.at[2], fb_recv.at[2], a_peer(i))
-
-    wait(fb_chunks, fb_recv.at[2])
+        force_bias = force_bias + fb_two[i].astype(jnp.float32)
     loads[4].wait()
-    fields = noise[...] - time_root * fb_all[...]
+    fields = noise[...] - time_root * force_bias
     fields_ref[...] = fields
     scaled = (-time_root * fields).astype(jnp.bfloat16)
 
@@ -363,8 +354,8 @@
     for j in range(nb):
         out_ref[:, j * electrons : (j + 1) * electrons] = landed[j, :, :electrons]
 
-    for i in range(3):
-        wait(fb_chunks, fb_send.at[i])
+    wait(fb_one.at[pl.ds(0, na - 1)], fb_send.at[0])
+    wait(fb_two.at[pl.ds(0, nb - 1)], fb_send.at[1])
     wait(phi.at[pl.ds(0, nb - 1)], phi_sem.at[0])
     for k in range(ORDER):
         wait(terms.at[k, :, pl.ds(0, (na - 1) * block)], term_send.at[k])
@@ -411,9 +402,8 @@
             pltpu.VMEM((orbitals, orbitals), bf16),
             pltpu.VMEM((walker_count, depth), f32),
             pltpu.VMEM((2, nb * rows, depth), bf16),
-            pltpu.VMEM((na, 8, LANES), f32),
-            pltpu.VMEM((nb, 8, LANES), f32),
-            pltpu.VMEM((walker_count, vectors), f32),
+            pltpu.VMEM((na, walker_count, vectors), bf16),
+            pltpu.VMEM((nb, walker_count, vectors), bf16),
             pltpu.VMEM((nb, rows, wide_electrons), bf16),
             pltpu.VMEM((ORDER, padded, orbitals), bf16),
             pltpu.VMEM(piece, bf16),
@@ -431,8 +421,8 @@
             pltpu.VMEM((nb, rows, wide_electrons), bf16),
             pltpu.VMEM((nb, rows, wide_electrons), bf16),
             dma((5,)),
-            dma((3,)),
-            dma((3,)),
+            dma((2,)),
+            dma((2,)),
             dma((2,)),
             dma((ORDER,)),
             dma((ORDER, PARTS)),

time: 65.8 us -> 63.1 us (0.959)
  Pallas kernels: 63.8 us -> 61.1 us
    pallas_call x1, Pallas kernels: 63.8 us -> 61.1 us  [local(): pl.pallas_call(functools.partial(kernel, (na, nb, nh, rows, electrons)),...]
where the time goes in v2:
time: 63.1 us; the launch traced here: 63 us
  Pallas kernels  61.1 us (97%)
  local copies, waits for them, and re-layouts  1.23 us (2%)
  between operations  0.64 us (1%)
    pallas_call x1, Pallas kernels, local(): pl.pallas_call(functools.partial(kernel, (na, nb, nh, rows, electrons)),...  61.1 us

profile of v2, /device:TPU:1, one launch (start us, length us, event | category | flops | bytes accessed | tf_op | source)
XLA Modules:
  0.0 63.0 jit_solution(9107134332726443674)
XLA Ops:
  0.6 61.1 %shard_map.68 = (f32[32,256]{1,0:T(8,128)S(1)}, bf16[16,1200]{1,0:T(8,128)(2,1)S(1)}) custom-call(bf16[16,4800]{1,0:T(8,128)(2,1)} %walkers_hbm.1, bf16[150,32,150]{2,1,0:T(8,128)(2,1)} %bitcast.6, bf16[2400,256]{1,0:T(8,128)(2,1)} %bitcast.7, bf16[4096,1024]{1,0:T(8,128)(2,1)} %bitcast.5, f32[32,256]{1,0:T(8,128)} %noise_hbm.1), custom_call_target="tpu_custom_call" | custom-call | tf_op jit(solution)/shard_map/pallas_call | solution.py:382
  61.7 0.6 copy.9
  62.4 0.6 copy.10

commit v3 on v2

--- a/solution.py
+++ b/solution.py
@@ -129,8 +129,16 @@
         pltpu.make_async_copy(span, span, sem).wait()
 
     pairs = ((walkers_hbm, walkers), (inverse_hbm, inverse), (rotated_hbm, rotated), (chol_hbm, chol), (noise_hbm, noise))
+    early_f = ceil_to(electrons // 2, 16)
+    first_f, last_f = pl.ds(0, early_f), pl.ds(early_f, electrons - early_f)
+    pairs = (
+        (walkers_hbm, walkers),
+        (inverse_hbm.at[first_f], inverse.at[first_f]),
+        *pairs[2:],
+        (inverse_hbm.at[last_f], inverse.at[last_f]),
+    )
     loads = [pltpu.make_async_copy(src, dst, load_sem.at[i]) for i, (src, dst) in enumerate(pairs)]
-    for i in (1, 0, 2):
+    for i in (1, 5, 0, 2):
         loads[i].start()
 
     barrier = pltpu.get_barrier_semaphore()
@@ -165,6 +173,8 @@
         return jnp.dot(gather[:, : size * count], taken, preferred_element_type=jnp.float32).reshape(count, 8, electrons)
 
     for f in range(0, electrons, 16):
+        if f == early_f:
+            loads[5].wait()
         by_walker[:, f : f + 16, :] = jnp.concatenate([eight(f), eight(f + 8)], axis=1).astype(jnp.bfloat16)
     loads[0].wait()
     for w in range(count):
@@ -291,19 +301,20 @@
             multiply(0, store_far, spots[:1] if n == 0 else spots[1:])
         send(send_far.at[lower, :, here], far_left.at[:, :, here], far_send.at[0], far_recv.at[0, n], right)
         send(send_far.at[upper, :, here], far_right.at[:, :, here], far_send.at[1], far_recv.at[1, n], left)
-    build(1, (h + 1) % nh)
-    build(0, (h + nh - 1) % nh)
-    multiply(1, store_right, spots)
     build(1, h)
-    multiply(0, store_left, spots)
     multiply(1, store_own, spots)
+    for i in range(1, nb):
+        send(own.at[b_at(i)], op_own.at[b], own_send, own_recv, b_peer(i))
+    op_own[b] = own[b]
+    build(0, (h + 1) % nh)
+    build(1, (h + nh - 1) % nh)
+    multiply(0, store_right, spots)
+    multiply(1, store_left, spots)
+
     for j in range(half):
         k = half + j
         send(send_right.at[k], op_early.at[b], early_send, early_recv, owner(k, 1))
         send(send_left.at[j], op_early.at[b], early_send, early_recv, owner(j, nh - 1))
-    for i in range(1, nb):
-        send(own.at[b_at(i)], op_own.at[b], own_send, own_recv, b_peer(i))
-    op_own[b] = own[b]
 
     for n, here in enumerate(spots):
         wait(far_left.at[:, :, here], far_recv.at[0, n])
@@ -420,7 +431,7 @@
             pltpu.VMEM((nb * rows, orbitals), bf16),
             pltpu.VMEM((nb, rows, wide_electrons), bf16),
             pltpu.VMEM((nb, rows, wide_electrons), bf16),
-            dma((5,)),
+            dma((6,)),
             dma((2,)),
             dma((2,)),
             dma((2,)),

time: 63.1 us -> 62.9 us (level)
  no operation moved by 1% of the time
where the time goes in v3:
time: 62.9 us; the launch traced here: 62.8 us
  Pallas kernels  60.9 us (97%)
  local copies, waits for them, and re-layouts  1.23 us (2%)
  between operations  0.64 us (1%)
    pallas_call x1, Pallas kernels, local(): pl.pallas_call(functools.partial(kernel, (na, nb, nh, rows, electrons)),...  60.9 us

profile of v3, /device:TPU:1, one launch (start us, length us, event | category | flops | bytes accessed | tf_op | source)
XLA Modules:
  0.0 62.8 jit_solution(14360168638322352749)
XLA Ops:
  0.6 60.9 %shard_map.68 = (f32[32,256]{1,0:T(8,128)S(1)}, bf16[16,1200]{1,0:T(8,128)(2,1)S(1)}) custom-call(bf16[16,4800]{1,0:T(8,128)(2,1)} %walkers_hbm.1, bf16[150,32,150]{2,1,0:T(8,128)(2,1)} %bitcast.6, bf16[2400,256]{1,0:T(8,128)(2,1)} %bitcast.7, bf16[4096,1024]{1,0:T(8,128)(2,1)} %bitcast.5, f32[32,256]{1,0:T(8,128)} %noise_hbm.1), custom_call_target="tpu_custom_call" | custom-call | tf_op jit(solution)/shard_map/pallas_call | solution.py:393
  61.5 0.6 copy.9
  62.2 0.6 copy.10
